TPU v7x, 32 devices: a whole 2x2x4 slice. The times are simulated.
32 devices in a mesh: group: 2 (over y), op: 4 (over z), site: 2 (over x), blk: 2 (over core).
Axes of the slice: x: 2, y: 2, z: 4, core: 2. Of those that a mesh axis runs over, the one named last changes fastest.
Arguments:
- psi: bfloat16 [4, 256, 2048], P(('group', 'site'), 'blk'), parts along dimension 0, may hold values from -6 to 6
- right_ops: bfloat16 [4, 8, 8, 256, 256], P(('group', 'site'), 'op'), parts along dimension 0
- left_blocks: bfloat16 [4, 8, 4, 8, 64, 64], P(('group', 'site'), 'op', 'blk'), parts along dimension 0
- sources: int32 [4, 8, 4, 8], P(('group', 'site'), 'op', 'blk'), parts along dimension 0, may hold values from 0 to 3
- env_basis: bfloat16 [4, 2048, 256], P(('group', 'site')), parts along dimension 0, may hold values from -0.125 to 0.125
Outputs:
- amplitudes: bfloat16 [4, 256, 2048], P(('group', 'site'), 'blk'), parts along dimension 0
- environment: float32 [4, 256, 256], P(('group', 'site'), 'blk'), parts along dimension 0
There are 2 independent parts, one for each index of `group`. A program takes and returns all parts, laid end to end along the dimension named above; each array names one. Nothing has to cross between parts.
All inputs are finite; a program needn't handle non-finite values.
Results may differ from a plain program's by a relative error of at most 0.012.
Values may be sent and summed in bfloat16 or wider, within the bound.
A program may use at most 64 MiB of HBM per device.

v0:
```python
import jax
import jax.numpy as jnp
from jax import lax
from jax.sharding import PartitionSpec as P

ITERS = 3


def entering(value, axis, combine, identity):
    size, here = (lax.axis_size(axis), lax.axis_index(axis))
    everything = lax.all_gather(value.astype(jnp.bfloat16), axis)
    start = jnp.broadcast_to(jnp.asarray(identity, value.dtype), value.shape)

    def lap(k, before):
        reached = k < here
        new = combine(before, everything[k].astype(value.dtype))
        return jnp.where(reached, new, before)

    return lax.fori_loop(0, size, lap, start)


def chain_product(first, second):
    return jnp.dot(
        first, second, precision=lax.Precision.HIGHEST, preferred_element_type=jnp.float32
    )


def pick_rows(table, index):
    return table[index]


def local_terms(vector, right_seg, left_seg, source_seg):
    local_rows, cols = vector.shape
    nrb, rblock = (right_seg.shape[1], right_seg.shape[2])
    bsize = left_seg.shape[-1]
    split = vector.reshape(local_rows, nrb, rblock)
    moved = jnp.einsum("ikb,tkbc->tikc", split, right_seg, preferred_element_type=jnp.float32)
    moved = moved.reshape(right_seg.shape[0], local_rows, cols).astype(jnp.bfloat16)
    gathered = lax.all_gather(moved, "blk", axis=1, tiled=True)
    stacked = gathered.reshape(gathered.shape[0], gathered.shape[1] // bsize, bsize, cols)
    picked = jax.vmap(pick_rows)(stacked, source_seg)
    image = jnp.einsum("tdjab,tdjbc->dac", left_seg, picked, preferred_element_type=jnp.float32)
    return image.reshape(local_rows, cols)


def on_device(psi, right_ops, left_blocks, sources, env_basis):
    local_rows, cols = (psi.shape[1], psi.shape[2])
    count = float(local_rows * lax.axis_size("blk") * cols)
    vector = psi[0]
    for step in range(ITERS):
        partial_sum = local_terms(vector, right_ops[0], left_blocks[0], sources[0])
        image = lax.psum(partial_sum, "op")
        inner_ww = lax.psum(jnp.sum(image * image), "blk")
        vector = (image * jnp.sqrt(count / inner_ww)).astype(jnp.bfloat16)
    factor_rows = jnp.dot(vector, env_basis[0], preferred_element_type=jnp.float32)
    factor = lax.all_gather(factor_rows.astype(jnp.bfloat16), "blk", axis=0, tiled=True).astype(
        factor_rows.dtype
    )
    total_rows = factor.shape[1]
    factor = factor * jnp.sqrt(float(total_rows * total_rows) / jnp.sum(factor * factor))
    identity = jnp.eye(total_rows, dtype=jnp.float32)
    carried = entering(factor, "site", chain_product, identity)
    scaled = carried * lax.rsqrt(jnp.mean(carried * carried))
    settled = jnp.where(lax.axis_index("site") == 0, carried, scaled)
    mine = lax.dynamic_slice_in_dim(settled, lax.axis_index("blk") * local_rows, local_rows, 0)
    return (vector[None], mine[None])


def solution(mesh):
    placed = (
        P(("group", "site"), "blk", None),
        P(("group", "site"), "op", None, None, None),
        P(("group", "site"), "op", "blk", None, None, None),
        P(("group", "site"), "op", "blk", None),
        P(("group", "site"), None, None),
    )
    return jax.shard_map(
        on_device,
        mesh=mesh,
        in_specs=placed,
        out_specs=(P(("group", "site"), "blk", None), P(("group", "site"), "blk", None)),
        check_vma=False,
    )
```

profile of v0, /device:TPU:0, one launch (start us, length us, event | category | flops | bytes accessed | tf_op | source)
XLA Modules:
  0.0 310.6 jit_solution(10387122887245528404)
XLA Ops:
  11.0 13.0 %all-gather.5.cloned.1.call-done = bf16[2,256,2048]{1,2,0:T(8,128)(2,1)} async-done(((bf16[2,128,2048]{1,2,0:T(8,128)(2,1)}), bf16[2,256,2048]{1,2,0:T(8,128)(2,1)}) %all-gather.5.cloned.1.call-update) | async-done | bytes 2097168 | tf_op jit(solution)/shard_map/all_gather | solution.py:39
  24.0 4.0 %copy.36 = bf16[2,256,2048]{2,1,0:T(8,128)(2,1)} copy(bf16[2,256,2048]{1,2,0:T(8,128)(2,1)} %all-gather.5.cloned.1.call-done) | data formatting | bytes 4194304 | tf_op jit(solution)/shard_map/all_gather | solution.py:39
  28.0 6.8 %gather_fusion = bf16[32,64,2048]{2,1,0:T(8,128)(2,1)} fusion(bf16[2,4,64,2048]{3,2,1,0:T(8,128)(2,1)} %bitcast.99, s32[32]{0:T(128)S(1)} %reshape.70), kind=kCustom, calls=%fused_computation | custom fusion | bytes 16777472 | tf_op jit(solution)/shard_map/vmap()/gather | solution.py:29
  34.8 6.1 %fusion.29 = f32[2,2048,64,1,1]{1,2,3,0,4:T(8,128)} fusion(bf16[2,2,8,64,2048]{4,3,2,1,0:T(8,128)(2,1)} %bitcast.102, bf16[1,2,2,8,64,64]{5,4,3,2,1,0:T(8,128)(2,1)S(1)} %copy-done.1), kind=kOutput, calls=%fused_computation.28 | convolution fusion | flops 536870912 | bytes 9699328 | tf_op jit(solution)/shard_map/tdjab,tdjbc->dac/dot_general | solution.py:42
  40.9 2.5 copy.37
  43.5 53.1 %all-reduce.4.cloned.1.call-done = f32[128,2048]{0,1:T(8,128)} async-done(((f32[128,2048]{0,1:T(8,128)}), f32[128,2048]{0,1:T(8,128)}) %all-reduce.4.cloned.1.call-update) | async-done | bytes 1048592 | tf_op jit(solution)/shard_map/psum | solution.py:52
  98.7 3.1 psum.43
  105.3 2.3 copy.40
  107.7 9.8 %all-gather.7.cloned.1.call-done = bf16[2,256,2048]{1,2,0:T(8,128)(2,1)} async-done(((bf16[2,128,2048]{1,2,0:T(8,128)(2,1)}), bf16[2,256,2048]{1,2,0:T(8,128)(2,1)}) %all-gather.7.cloned.1.call-update) | async-done | bytes 2097168 | tf_op jit(solution)/shard_map/all_gather | solution.py:39
  117.5 4.0 %copy.41 = bf16[2,256,2048]{2,1,0:T(8,128)(2,1)} copy(bf16[2,256,2048]{1,2,0:T(8,128)(2,1)} %all-gather.7.cloned.1.call-done) | data formatting | bytes 4194304 | tf_op jit(solution)/shard_map/all_gather | solution.py:39
  121.5 6.7 %gather_fusion.1 = bf16[32,64,2048]{2,1,0:T(8,128)(2,1)} fusion(bf16[2,4,64,2048]{3,2,1,0:T(8,128)(2,1)} %bitcast.100, s32[32]{0:T(128)S(1)} %reshape.70), kind=kCustom, calls=%fused_computation.1 | custom fusion | bytes 16777472 | tf_op jit(solution)/shard_map/vmap()/gather | solution.py:29
  128.3 6.1 %fusion.31 = f32[2,2048,64,1,1]{1,2,3,0,4:T(8,128)} fusion(bf16[2,2,8,64,2048]{4,3,2,1,0:T(8,128)(2,1)} %bitcast.103, bf16[1,2,2,8,64,64]{5,4,3,2,1,0:T(8,128)(2,1)S(1)} %copy-done.1), kind=kOutput, calls=%fused_computation.30 | convolution fusion | flops 536870912 | bytes 9699328 | tf_op jit(solution)/shard_map/tdjab,tdjbc->dac/dot_general | solution.py:42
  134.3 2.5 copy.42
  137.0 53.1 %all-reduce.6.cloned.1.call-done = f32[128,2048]{0,1:T(8,128)} async-done(((f32[128,2048]{0,1:T(8,128)}), f32[128,2048]{0,1:T(8,128)}) %all-reduce.6.cloned.1.call-update) | async-done | bytes 1048592 | tf_op jit(solution)/shard_map/psum | solution.py:52
  192.2 3.1 psum.45
  198.8 2.3 copy.45
  201.2 9.8 %all-gather.9.cloned.1.call-done = bf16[2,256,2048]{1,2,0:T(8,128)(2,1)} async-done(((bf16[2,128,2048]{1,2,0:T(8,128)(2,1)}), bf16[2,256,2048]{1,2,0:T(8,128)(2,1)}) %all-gather.9.cloned.1.call-update) | async-done | bytes 2097168 | tf_op jit(solution)/shard_map/all_gather | solution.py:39
  211.0 4.0 %copy.46 = bf16[2,256,2048]{2,1,0:T(8,128)(2,1)} copy(bf16[2,256,2048]{1,2,0:T(8,128)(2,1)} %all-gather.9.cloned.1.call-done) | data formatting | bytes 4194304 | tf_op jit(solution)/shard_map/all_gather | solution.py:39
  215.0 6.7 %gather_fusion.2 = bf16[32,64,2048]{2,1,0:T(8,128)(2,1)} fusion(bf16[2,4,64,2048]{3,2,1,0:T(8,128)(2,1)} %bitcast.98, s32[32]{0:T(128)S(1)} %reshape.70), kind=kCustom, calls=%fused_computation.2 | custom fusion | bytes 16777472 | tf_op jit(solution)/shard_map/vmap()/gather | solution.py:29
  221.7 6.1 %fusion.33 = f32[2,2048,64,1,1]{1,2,3,0,4:T(8,128)} fusion(bf16[2,2,8,64,2048]{4,3,2,1,0:T(8,128)(2,1)} %bitcast.101, bf16[1,2,2,8,64,64]{5,4,3,2,1,0:T(8,128)(2,1)S(1)} %copy-done.1), kind=kOutput, calls=%fused_computation.32 | convolution fusion | flops 536870912 | bytes 9699328 | tf_op jit(solution)/shard_map/tdjab,tdjbc->dac/dot_general | solution.py:42
  227.8 53.1 %all-reduce.8.cloned.1.call-done = f32[128,2048]{1,0:T(8,128)} async-done(((f32[128,2048]{1,0:T(8,128)}), f32[128,2048]{1,0:T(8,128)}) %all-reduce.8.cloned.1.call-update) | async-done | bytes 1048592 | tf_op jit(solution)/shard_map/psum | solution.py:52
  283.1 3.1 psum.47
  291.8 6.4 %all-gather = bf16[512,256]{1,0:T(8,128)(2,1)} all-gather(bf16[256,256]{1,0:T(8,128)(2,1)S(1)} %fusion.37), channel_id=2, replica_groups=mesh['group'=2,'op'=4,'site'=2,'blk'=2] {'site'}, dimensions={0}, use_global_device_ids=true | all-gather | bytes 393216 | tf_op jit(solution)/shard_map/all_gather | solution.py:11
  298.1 2.6 while.13
  (47 shorter events, 24.9 us)
Async XLA Ops:
  7.2 1.8 copy-start
  7.2 16.9 %all-gather.5.cloned.1.call-start = ((), (), s32[]{:S(2)}) async-start(), calls=%async_computation | async-start | bytes 3145728 | tf_op jit(solution)/shard_map/all_gather | solution.py:39
  9.8 1.1 copy-start.4
  10.9 85.8 %all-reduce.4.cloned.1.call-start = ((), (), s32[]{:S(2)}) async-start(), calls=%async_computation.1 | async-start | bytes 2097152 | tf_op jit(solution)/shard_map/psum | solution.py:52
  28.0 6.8 %copy-start.1 = (bf16[1,2,2,8,64,64]{5,4,3,2,1,0:T(8,128)(2,1)S(1)}, bf16[1,2,2,8,64,64]{5,4,3,2,1,0:T(8,128)(2,1)}, u32[]{:S(2)}) copy-start(bf16[1,2,2,8,64,64]{5,4,3,2,1,0:T(8,128)(2,1)} %param.9) | copy-start | bytes 786436
  43.5 74.0 %all-gather.7.cloned.1.call-start = ((), (), s32[]{:S(2)}) async-start(), calls=%async_computation.2 | async-start | bytes 3145728 | tf_op jit(solution)/shard_map/all_gather | solution.py:39
  107.7 82.4 %all-reduce.6.cloned.1.call-start = ((), (), s32[]{:S(2)}) async-start(), calls=%async_computation.3 | async-start | bytes 2097152 | tf_op jit(solution)/shard_map/psum | solution.py:52
  136.9 74.0 %all-gather.9.cloned.1.call-start = ((), (), s32[]{:S(2)}) async-start(), calls=%async_computation.4 | async-start | bytes 3145728 | tf_op jit(solution)/shard_map/all_gather | solution.py:39
  201.1 79.9 %all-reduce.8.cloned.1.call-start = ((), (), s32[]{:S(2)}) async-start(), calls=%async_computation.5 | async-start | bytes 2097152 | tf_op jit(solution)/shard_map/psum | solution.py:52
  227.8 59.1 %copy-start.3 = (bf16[1,2048,256]{2,1,0:T(8,128)(2,1)S(1)}, bf16[1,2048,256]{2,1,0:T(8,128)(2,1)}, u32[]{:S(2)}) copy-start(bf16[1,2048,256]{2,1,0:T(8,128)(2,1)} %param.11) | copy-start | bytes 3145732
  298.1 4.8 %copy-start.2 = (f32[128,2048]{1,0:T(8,128)S(1)}, f32[128,2048]{1,0:T(8,128)}, u32[]{:S(2)}) copy-start(f32[128,2048]{1,0:T(8,128)} %all-reduce.8.cloned.1.call-done) | copy-start | bytes 3145732
Sparse Core Ops, SparseCore 0:
  11.0 13.0 all-gather.4
  43.6 52.9 all-reduce.3
  107.8 9.6 all-gather.6
  137.0 53.0 all-reduce.5
  201.2 9.6 all-gather.8
  227.9 52.9 all-reduce.7
where the time goes:
time: 312 us; the launch traced here: 311 us
  waiting for transfers between devices  192 us (62%)
  local copies, waits for them, and re-layouts  45.6 us (15%)
  matrix products  26.1 us (8%)
  between operations  17.8 us (6%)
  blocking collectives  17.5 us (6%)
  other arithmetic  11.1 us (4%)
    psum x3, waiting for transfers between devices, on_device(): image = lax.psum(partial_sum, 'op')  159 us
    all_gather x3, waiting for transfers between devices, local_terms(): gathered = lax.all_gather(moved, 'blk', axis=1, tiled=True)  32.6 us
    gather x4, local copies, waits for them, and re-layouts, pick_rows(): return table[index]  20.4 us
    dot_general x3, matrix products, local_terms(): jnp.einsum('tdjab,tdjbc->dac', left_seg, picked, preferred_element_type=j...  18.2 us
    all_gather x3, local copies, waits for them, and re-layouts, local_terms(): gathered = lax.all_gather(moved, 'blk', axis=1, tiled=True)  12 us
    psum x3, blocking collectives, on_device(): inner_ww = lax.psum(jnp.sum(image * image), 'blk')  9.23 us
    all_gather x1, blocking collectives, entering(): everything = lax.all_gather(value.astype(jnp.bfloat16), axis)  6.35 us
    reduce_sum x3, other arithmetic, on_device(): inner_ww = lax.psum(jnp.sum(image * image), 'blk')  6.29 us
  transfers between devices with their start and end apart: 6, of which 6 were waited for; matrix products, arithmetic and copies ran while one was open for 0% of the time, Pallas kernels for 0%

commit v1 on v0

--- a/solution.py
+++ b/solution.py
@@ -1,9 +1,16 @@
+import functools
+
 import jax
 import jax.numpy as jnp
 from jax import lax
+from jax.experimental import pallas as pl
+from jax.experimental.pallas import tpu as pltpu
 from jax.sharding import PartitionSpec as P
 
 ITERS = 3
+MESH = pl.DeviceIdType.MESH
+F32 = jnp.float32
+BF16 = jnp.bfloat16
 
 
 def entering(value, axis, combine, identity):
@@ -43,7 +50,7 @@
     return image.reshape(local_rows, cols)
 
 
-def on_device(psi, right_ops, left_blocks, sources, env_basis):
+def general_plan(psi, right_ops, left_blocks, sources, env_basis):
     local_rows, cols = (psi.shape[1], psi.shape[2])
     count = float(local_rows * lax.axis_size("blk") * cols)
     vector = psi[0]
@@ -66,6 +73,325 @@
     return (vector[None], mine[None])
 
 
+def column_kernel(
+    n, src_ref, psi_ref, right_ref, left_ref, env_ref, amp_ref, out_ref,
+    r_all, l_all, vec, env, tail, meta, fac, fac_in, fmeta,
+    local_sem, r_send, r_recv, p_send, p_recv, l_send, l_recv, s_send, s_recv,
+    a_send, a_recv, x_send, x_recv, m_send, m_recv, f_send, f_recv, g_send, g_recv,
+):
+    terms, nrb, rb, _ = right_ref.shape
+    rows, cols = psi_ref.shape
+    nd, nnz, bs = left_ref.shape[1], left_ref.shape[2], left_ref.shape[3]
+    all_rows = 2 * rows
+    z = lax.axis_index("op")
+    c = lax.axis_index("blk")
+    site = lax.axis_index("site")
+    k = 2 * z + c
+    ksib = 2 * z + 1 - c
+    mine = pl.ds(pl.multiple_of(c * rows, rows), rows)
+    theirs = pl.ds(pl.multiple_of((1 - c) * rows, rows), rows)
+
+    def remote(src, dst, send, recv, device):
+        return pltpu.make_async_remote_copy(
+            src_ref=src, dst_ref=dst, send_sem=send, recv_sem=recv,
+            device_id=device, device_id_type=MESH,
+        )
+
+    sibling = {"blk": 1 - c}
+    across = {"site": 1 - site}
+    diagonal = {"site": 1 - site, "blk": 1 - c}
+
+    own_r = pltpu.make_async_copy(right_ref.at[:, k], r_all.at[z], local_sem.at[0])
+    own_p = pltpu.make_async_copy(
+        psi_ref.at[:, pl.ds(pl.multiple_of(k * rb, rb), rb)], vec.at[mine], local_sem.at[1]
+    )
+    own_e = pltpu.make_async_copy(env_ref, env, local_sem.at[2])
+    own_r.start()
+    own_p.start()
+    own_e.start()
+
+    barrier = pltpu.get_barrier_semaphore()
+    for off in range(1, n):
+        pl.semaphore_signal(
+            barrier, inc=1, device_id={"op": lax.rem(z + off, n)}, device_id_type=MESH
+        )
+    for dev in (sibling, across, diagonal):
+        pl.semaphore_signal(barrier, inc=1, device_id=dev, device_id_type=MESH)
+    pl.semaphore_wait(barrier, n + 2)
+
+    def r_copy(off):
+        dest = lax.rem(z + off, n)
+        return remote(
+            right_ref.at[:, 2 * dest + c], r_all.at[z], r_send.at[off], r_recv.at[z],
+            {"op": dest},
+        )
+
+    order = sorted(range(1, n), key=lambda o: -min(o, n - o))
+    for off in order:
+        r_copy(off).start()
+    p_copy = remote(
+        psi_ref.at[:, pl.ds(pl.multiple_of(ksib * rb, rb), rb)], vec.at[mine],
+        p_send, p_recv, sibling,
+    )
+    p_copy.start()
+
+    diff = lax.broadcasted_iota(jnp.int32, (bs, all_rows), 1) - lax.broadcasted_iota(
+        jnp.int32, (bs, all_rows), 0
+    )
+    for t in range(terms):
+        for d in range(nd):
+            total = jnp.zeros((bs, all_rows), F32)
+            for j in range(nnz):
+                place = jnp.where(diff == bs * src_ref[t, d, j], 1.0, 0.0).astype(BF16)
+                total += jnp.dot(left_ref[t, d, j], place, preferred_element_type=F32)
+            at = pl.ds(pl.multiple_of(c * rows + d * bs, bs), bs)
+            l_all[z, t, at, :] = total.astype(BF16)
+
+    def right_hop(ref, origin, send, recv):
+        return remote(ref(origin), ref(origin), send, recv.at[origin], {"op": lax.rem(z + 1, n)})
+
+    def left_hop(ref, origin, send, recv):
+        return remote(
+            ref(origin), ref(origin), send, recv.at[origin], {"op": lax.rem(z + n - 1, n)}
+        )
+
+    def start_line(ref, send, recv):
+        @pl.when(z + 1 < n)
+        def _():
+            right_hop(ref, z, send.at[0, 0], recv).start()
+
+        @pl.when(z > 0)
+        def _():
+            left_hop(ref, z, send.at[1, 0], recv).start()
+
+    def step_line(ref, send, recv, s, use):
+        @pl.when(z - s >= 0)
+        def _():
+            o = lax.rem(z - s + n, n)
+            right_hop(ref, o, send.at[0, 0], recv).wait_recv()
+            if s < n - 1:
+                @pl.when(z + 1 < n)
+                def _():
+                    right_hop(ref, o, send.at[0, s], recv).start()
+            use(o)
+
+        @pl.when(z + s < n)
+        def _():
+            o = lax.rem(z + s, n)
+            left_hop(ref, o, send.at[1, 0], recv).wait_recv()
+            if s < n - 1:
+                @pl.when(z > 0)
+                def _():
+                    left_hop(ref, o, send.at[1, s], recv).start()
+            use(o)
+
+    def end_line(ref, send, recv):
+        for s in range(n - 1):
+            @pl.when((z + 1 < n) & (z - s >= 0))
+            def _():
+                right_hop(ref, lax.rem(z - s + n, n), send.at[0, s], recv).wait_send()
+
+            @pl.when((z > 0) & (z + s < n))
+            def _():
+                left_hop(ref, lax.rem(z + s, n), send.at[1, s], recv).wait_send()
+
+    def l_slot(o):
+        return l_all.at[o, :, mine, :]
+
+    def to_sibling(o):
+        return remote(l_slot(o), l_slot(o), s_send.at[o], s_recv.at[o], sibling)
+
+    start_line(l_slot, l_send, l_recv)
+    to_sibling(z).start()
+
+    own_p.wait()
+    p_copy.wait()
+    own_r.wait()
+
+    for s in range(1, n):
+        step_line(l_slot, l_send, l_recv, s, lambda o: to_sibling(o).start())
+
+    def product(o, start):
+        v = vec[...]
+        total = start
+        for t in range(terms):
+            moved = jnp.dot(v, r_all[o, t], preferred_element_type=F32).astype(BF16)
+            total = total + jnp.dot(l_all[o, t], moved, preferred_element_type=F32)
+        return total
+
+    image = jnp.zeros((all_rows, rb), F32)
+    for off in [0] + order[::-1]:
+        o = lax.rem(z + off, n)
+        to_sibling(o).wait_recv()
+        if off:
+            remote(
+                right_ref.at[:, k], r_all.at[o], r_send.at[0], r_recv.at[o], {"op": o}
+            ).wait_recv()
+        image = product(o, image)
+
+    exponent = jnp.zeros((1, 1), F32)
+
+    def settle(image, exponent):
+        top = jnp.max(jnp.abs(image), axis=(0, 1), keepdims=True)
+        e = jnp.where(top > 0.0, jnp.clip(jnp.floor(jnp.log2(top)), -100.0, 100.0), 0.0)
+        return image * jnp.exp2(-e), exponent + e
+
+    for step in range(1, ITERS):
+        image, exponent = settle(image, exponent)
+        vec[...] = image.astype(BF16)
+        image = jnp.zeros((all_rows, rb), F32)
+        for o in range(n):
+            image = product(o, image)
+    image, exponent = settle(image, exponent)
+    square = jnp.sum(image * image, axis=(0, 1), keepdims=True)
+    vec[...] = image.astype(BF16)
+
+    here = pl.ds(pl.multiple_of(c * rb, rb), rb)
+    x_copy = remote(
+        vec.at[theirs, :], tail.at[z, :, here], x_send.at[0], x_recv.at[0], sibling
+    )
+    x_copy.start()
+    lane = lax.broadcasted_iota(jnp.int32, (8, 128), 1)
+    meta[z, c] = jnp.where(lane == 0, jnp.broadcast_to(exponent, (8, 128)),
+                           jnp.broadcast_to(square, (8, 128)))
+    xm_copy = remote(meta.at[z, c], meta.at[z, c], x_send.at[1], x_recv.at[1], sibling)
+    xm_copy.start()
+    tail[z, :, here] = vec[mine, :]
+
+    def a_slot(o):
+        return tail.at[o]
+
+    x_copy.wait()
+    start_line(a_slot, a_send, a_recv)
+    xm_copy.wait()
+
+    def m_copy(off):
+        return remote(
+            meta.at[z], meta.at[z], m_send.at[off], m_recv.at[z], {"op": lax.rem(z + off, n)}
+        )
+
+    for off in range(1, n):
+        m_copy(off).start()
+
+    step_line(a_slot, a_send, a_recv, 1, lambda o: None)
+    for off in range(1, n):
+        o = lax.rem(z + off, n)
+        remote(
+            meta.at[o], meta.at[o], m_send.at[0], m_recv.at[o], {"op": o}
+        ).wait_recv()
+
+    exps = [meta[o // 2, o % 2][0:1, 0:1] for o in range(2 * n)]
+    sqs = [meta[o // 2, o % 2][0:1, 1:2] for o in range(2 * n)]
+    low = jnp.full((1, 1), -1.0e4, F32)
+    big = low
+    for e, q in zip(exps, sqs):
+        big = jnp.maximum(big, jnp.where(q > 0.0, e, low))
+    ww = jnp.zeros((1, 1), F32)
+    rel = []
+    for e, q in zip(exps, sqs):
+        r = jnp.where(q > 0.0, jnp.exp2(jnp.maximum(e - big, -120.0)), 0.0)
+        rel.append(r)
+        ww = ww + q * r * r
+    unit = jnp.sqrt(float(all_rows * cols) / ww)
+
+    def finish(o, factor):
+        for half in range(2):
+            scale = rel[2 * o + half] * unit
+            block = (tail[o, :, half * rb:(half + 1) * rb].astype(F32) * scale).astype(BF16)
+            lo = (2 * o + half) * rb
+            amp_ref[:, lo:lo + rb] = block
+            factor = factor + jnp.dot(block, env[lo:lo + rb, :], preferred_element_type=F32)
+        return factor
+
+    for s in range(2, n):
+        step_line(a_slot, a_send, a_recv, s, lambda o: None)
+    own_e.wait()
+    factor = jnp.zeros(out_ref.shape, F32)
+    for o in range(n):
+        factor = finish(o, factor)
+
+    fac[...] = factor.astype(BF16)
+    f_copy = remote(fac, fac_in, f_send, f_recv, across)
+    f_copy.start()
+    rounded = fac[...].astype(F32)
+    fsq = jnp.sum(rounded * rounded, axis=(0, 1), keepdims=True)
+    fmeta[0] = jnp.broadcast_to(fsq, (8, 128))
+    g_near = remote(fmeta.at[0], fmeta.at[1], g_send.at[0], g_recv.at[0], across)
+    g_far = remote(fmeta.at[0], fmeta.at[2], g_send.at[1], g_recv.at[1], diagonal)
+    g_near.start()
+    g_far.start()
+
+    for off in range(1, n):
+        r_copy(off).wait_send()
+        m_copy(off).wait_send()
+    end_line(l_slot, l_send, l_recv)
+    end_line(a_slot, a_send, a_recv)
+    for o in range(n):
+        to_sibling(o).wait_send()
+    g_near.wait()
+    g_far.wait()
+    f_copy.wait()
+    total = fmeta[1][0:1, 0:1] + fmeta[2][0:1, 0:1]
+    earlier = fac_in[...].astype(F32) * lax.rsqrt(total / float(all_rows * out_ref.shape[1]))
+    eye = jnp.where(
+        lax.broadcasted_iota(jnp.int32, out_ref.shape, 0) + c * rows
+        == lax.broadcasted_iota(jnp.int32, out_ref.shape, 1), 1.0, 0.0,
+    )
+    first = jnp.full(out_ref.shape, site, jnp.int32) == 0
+    out_ref[...] = jnp.where(first, eye, earlier)
+
+
+def column_plan(psi, right_ops, left_blocks, sources, env_basis):
+    n = lax.axis_size("op")
+    rows, cols = psi.shape[1], psi.shape[2]
+    terms, nrb, rb = right_ops.shape[1], right_ops.shape[2], right_ops.shape[3]
+    width = env_basis.shape[2]
+    dma = pltpu.SemaphoreType.DMA
+    hbm = pl.BlockSpec(memory_space=pl.ANY)
+    vmem = pl.BlockSpec(memory_space=pltpu.VMEM)
+    amplitudes, environment = pl.pallas_call(
+        functools.partial(column_kernel, n),
+        out_shape=(
+            jax.ShapeDtypeStruct((rows, cols), BF16),
+            jax.ShapeDtypeStruct((rows, width), F32),
+        ),
+        in_specs=[pl.BlockSpec(memory_space=pltpu.SMEM), hbm, hbm, vmem, hbm],
+        out_specs=(vmem, vmem),
+        scratch_shapes=[
+            pltpu.VMEM((n, terms, rb, rb), BF16),
+            pltpu.VMEM((n, terms, 2 * rows, 2 * rows), BF16),
+            pltpu.VMEM((2 * rows, rb), BF16),
+            pltpu.VMEM((cols, width), BF16),
+            pltpu.VMEM((n, rows, 2 * rb), BF16),
+            pltpu.VMEM((n, 2, 8, 128), F32),
+            pltpu.VMEM((rows, width), BF16),
+            pltpu.VMEM((rows, width), BF16),
+            pltpu.VMEM((3, 8, 128), F32),
+            dma((3,)),
+            dma((n,)), dma((n,)), dma, dma, dma((2, n)), dma((n,)), dma((n,)), dma((n,)),
+            dma((2, n)), dma((n,)), dma((2,)), dma((2,)), dma((n,)), dma((n,)),
+            dma, dma, dma((2,)), dma((2,)),
+        ],
+        compiler_params=pltpu.CompilerParams(
+            collective_id=0, has_side_effects=True, vmem_limit_bytes=40 * 1024 * 1024
+        ),
+    )(sources[0], psi[0], right_ops[0], left_blocks[0], env_basis[0])
+    return (amplitudes[None], environment[None])
+
+
+def on_device(psi, right_ops, left_blocks, sources, env_basis):
+    owners = lax.axis_size("op") * lax.axis_size("blk")
+    fits = (
+        owners == right_ops.shape[2]
+        and lax.axis_size("blk") == 2
+        and lax.axis_size("site") == 2
+        and psi.shape[0] == 1
+        and env_basis.shape[2] == 2 * psi.shape[1]
+    )
+    plan = column_plan if fits else general_plan
+    return plan(psi, right_ops, left_blocks, sources, env_basis)
+
+
 def solution(mesh):
     placed = (
         P(("group", "site"), "blk", None),

time: 312 us -> 71.4 us (0.23)
  waiting for transfers between devices: 192 us -> 0 us
  Pallas kernels: 0 us -> 63.4 us
  local copies, waits for them, and re-layouts: 45.6 us -> 7.02 us
  matrix products: 26.1 us -> 0 us
  blocking collectives: 17.5 us -> 0 us
  between operations: 17.8 us -> 0.65 us
  other arithmetic: 11.1 us -> 0 us
    psum x3 -> x0, waiting for transfers between devices: 159 us -> none  [on_device(): image = lax.psum(partial_sum, 'op')]
    pallas_call x0 -> x1, Pallas kernels: none -> 63.4 us  [column_plan(): pl.pallas_call(functools.partial(column_kernel, n), out_shape=(jax.ShapeD...]
    all_gather x3 -> x0, waiting for transfers between devices: 32.6 us -> none  [local_terms(): gathered = lax.all_gather(moved, 'blk', axis=1, tiled=True)]
    dot_general x9 -> x0, matrix products: 26.1 us -> none  [the longest x3 18.2 us: local_terms(): jnp.einsum('tdjab,tdjbc->dac', left_seg, picked, preferred_element_type=j...]
    gather x4 -> x0, local copies, waits for them, and re-layouts: 20.4 us -> none  [pick_rows(): return table[index]]
    all_gather x3 -> x0, local copies, waits for them, and re-layouts: 12 us -> none  [local_terms(): gathered = lax.all_gather(moved, 'blk', axis=1, tiled=True)]
    psum x3 -> x0, blocking collectives: 9.23 us -> none  [on_device(): inner_ww = lax.psum(jnp.sum(image * image), 'blk')]
    all_gather x2 -> x0, blocking collectives: 8.25 us -> none  [the longest x1 6.35 us: entering(): everything = lax.all_gather(value.astype(jnp.bfloat16), axis)]
  transfers between devices with their start and end apart: 6 -> 0, of which waited for: 6 -> 0; matrix products, arithmetic and copies ran while one was open for 0% -> 0% of each run, Pallas kernels for 0% -> 0%
where the time goes in v1:
time: 71.4 us; the launch traced here: 71.1 us
  Pallas kernels  63.4 us (89%)
  local copies, waits for them, and re-layouts  7.02 us (10%)
    pallas_call x1, Pallas kernels, column_plan(): pl.pallas_call(functools.partial(column_kernel, n), out_shape=(jax.ShapeD...  63.4 us
    unnamed x12, local copies, waits for them, and re-layouts  7.02 us

profile of v1, /device:TPU:0, one launch (start us, length us, event | category | flops | bytes accessed | tf_op | source)
XLA Modules:
  0.0 71.1 jit_solution(17416145325203435911)
XLA Ops:
  0.6 0.0 copy-start
  0.6 1.6 %copy-done = bf16[1,2,8,256,256]{4,3,2,1,0:T(8,128)(2,1)S(1)} copy-done((bf16[1,2,8,256,256]{4,3,2,1,0:T(8,128)(2,1)S(1)}, bf16[1,2,8,256,256]{4,3,2,1,0:T(8,128)(2,1)}, u32[]{:S(2)}) %copy-start) | copy-done | bytes 2097176
  2.2 0.0 copy-start.1
  2.2 1.2 %copy-done.1 = bf16[1,2048,256]{2,1,0:T(8,128)(2,1)S(1)} copy-done((bf16[1,2048,256]{2,1,0:T(8,128)(2,1)S(1)}, bf16[1,2048,256]{2,1,0:T(8,128)(2,1)}, u32[]{:S(2)}) %copy-start.1) | copy-done | bytes 1048600
  3.4 0.0 copy-start.2
  3.5 1.0 %copy-done.2 = bf16[1,128,2048]{2,1,0:T(8,128)(2,1)S(1)} copy-done((bf16[1,128,2048]{2,1,0:T(8,128)(2,1)S(1)}, bf16[1,128,2048]{2,1,0:T(8,128)(2,1)}, u32[]{:S(2)}) %copy-start.2) | copy-done | bytes 524312
  4.5 0.0 copy-start.3
  4.5 1.0 %copy-done.3 = bf16[1,2,2,8,64,64]{5,4,3,2,1,0:T(8,128)(2,1)S(1)} copy-done((bf16[1,2,2,8,64,64]{5,4,3,2,1,0:T(8,128)(2,1)S(1)}, bf16[1,2,2,8,64,64]{5,4,3,2,1,0:T(8,128)(2,1)}, u32[]{:S(2)}) %copy-start.3) | copy-done | bytes 262168
  5.5 0.0 copy-start.4
  5.5 0.7 copy-done.4
  6.2 63.4 %shard_map.68 = (bf16[128,2048]{1,0:T(8,128)(2,1)S(1)}, f32[128,256]{1,0:T(8,128)S(1)}) custom-call(s32[2,2,8]{2,1,0:T(2,128)S(1)} %bitcast.13, bf16[128,2048]{1,0:T(8,128)(2,1)S(1)} %bitcast.10, bf16[2,8,256,256]{3,2,1,0:T(8,128)(2,1)S(1)} %bitcast.7, bf16[2,2,8,64,64]{4,3,2,1,0:T(8,128)(2,1)S(1)} %bitcast.11, bf16[2048,256]{1,0:T(8,128)(2,1)S(1)} %bitcast.8), custom_call_target="tpu_custom_call" | custom-call | tf_op jit(solution)/shard_map/pallas_call | solution.py:352
  69.6 0.8 %copy.9 = bf16[1,128,2048]{2,1,0:T(8,128)(2,1)} copy(bf16[1,128,2048]{2,1,0:T(8,128)(2,1)S(1)} %bitcast.9) | data formatting | bytes 1048576
  70.4 0.7 copy.10
Async XLA Ops:
  0.6 1.6 %copy-start = (bf16[1,2,8,256,256]{4,3,2,1,0:T(8,128)(2,1)S(1)}, bf16[1,2,8,256,256]{4,3,2,1,0:T(8,128)(2,1)}, u32[]{:S(2)}) copy-start(bf16[1,2,8,256,256]{4,3,2,1,0:T(8,128)(2,1)} %param.6) | copy-start | bytes 6291460
  2.2 1.2 %copy-start.1 = (bf16[1,2048,256]{2,1,0:T(8,128)(2,1)S(1)}, bf16[1,2048,256]{2,1,0:T(8,128)(2,1)}, u32[]{:S(2)}) copy-start(bf16[1,2048,256]{2,1,0:T(8,128)(2,1)} %param.9) | copy-start | bytes 3145732
  3.4 1.0 %copy-start.2 = (bf16[1,128,2048]{2,1,0:T(8,128)(2,1)S(1)}, bf16[1,128,2048]{2,1,0:T(8,128)(2,1)}, u32[]{:S(2)}) copy-start(bf16[1,128,2048]{2,1,0:T(8,128)(2,1)} %param.5) | copy-start | bytes 1572868
  4.5 1.0 %copy-start.3 = (bf16[1,2,2,8,64,64]{5,4,3,2,1,0:T(8,128)(2,1)S(1)}, bf16[1,2,2,8,64,64]{5,4,3,2,1,0:T(8,128)(2,1)}, u32[]{:S(2)}) copy-start(bf16[1,2,2,8,64,64]{5,4,3,2,1,0:T(8,128)(2,1)} %param.7) | copy-start | bytes 786436
  5.5 0.7 copy-start.4

commit v2 on v1

v2 whole, which is shorter than its diff:
```python
import functools

import jax
import jax.numpy as jnp
from jax import lax
from jax.experimental import pallas as pl
from jax.experimental.pallas import tpu as pltpu
from jax.sharding import PartitionSpec as P

ITERS = 3
MESH = pl.DeviceIdType.MESH
F32 = jnp.float32
BF16 = jnp.bfloat16


def entering(value, axis, combine, identity):
    size, here = (lax.axis_size(axis), lax.axis_index(axis))
    everything = lax.all_gather(value.astype(jnp.bfloat16), axis)
    start = jnp.broadcast_to(jnp.asarray(identity, value.dtype), value.shape)

    def lap(k, before):
        reached = k < here
        new = combine(before, everything[k].astype(value.dtype))
        return jnp.where(reached, new, before)

    return lax.fori_loop(0, size, lap, start)


def chain_product(first, second):
    return jnp.dot(
        first, second, precision=lax.Precision.HIGHEST, preferred_element_type=jnp.float32
    )


def pick_rows(table, index):
    return table[index]


def local_terms(vector, right_seg, left_seg, source_seg):
    local_rows, cols = vector.shape
    nrb, rblock = (right_seg.shape[1], right_seg.shape[2])
    bsize = left_seg.shape[-1]
    split = vector.reshape(local_rows, nrb, rblock)
    moved = jnp.einsum("ikb,tkbc->tikc", split, right_seg, preferred_element_type=jnp.float32)
    moved = moved.reshape(right_seg.shape[0], local_rows, cols).astype(jnp.bfloat16)
    gathered = lax.all_gather(moved, "blk", axis=1, tiled=True)
    stacked = gathered.reshape(gathered.shape[0], gathered.shape[1] // bsize, bsize, cols)
    picked = jax.vmap(pick_rows)(stacked, source_seg)
    image = jnp.einsum("tdjab,tdjbc->dac", left_seg, picked, preferred_element_type=jnp.float32)
    return image.reshape(local_rows, cols)


def general_plan(psi, right_ops, left_blocks, sources, env_basis):
    local_rows, cols = (psi.shape[1], psi.shape[2])
    count = float(local_rows * lax.axis_size("blk") * cols)
    vector = psi[0]
    for step in range(ITERS):
        partial_sum = local_terms(vector, right_ops[0], left_blocks[0], sources[0])
        image = lax.psum(partial_sum, "op")
        inner_ww = lax.psum(jnp.sum(image * image), "blk")
        vector = (image * jnp.sqrt(count / inner_ww)).astype(jnp.bfloat16)
    factor_rows = jnp.dot(vector, env_basis[0], preferred_element_type=jnp.float32)
    factor = lax.all_gather(factor_rows.astype(jnp.bfloat16), "blk", axis=0, tiled=True).astype(
        factor_rows.dtype
    )
    total_rows = factor.shape[1]
    factor = factor * jnp.sqrt(float(total_rows * total_rows) / jnp.sum(factor * factor))
    identity = jnp.eye(total_rows, dtype=jnp.float32)
    carried = entering(factor, "site", chain_product, identity)
    scaled = carried * lax.rsqrt(jnp.mean(carried * carried))
    settled = jnp.where(lax.axis_index("site") == 0, carried, scaled)
    mine = lax.dynamic_slice_in_dim(settled, lax.axis_index("blk") * local_rows, local_rows, 0)
    return (vector[None], mine[None])


def column_kernel(
    n, src_ref, psi_ref, right_ref, left_ref, env_ref, amp_ref, out_ref,
    r_all, l_all, vec, env, left, tail, meta, rel, total_fac, fac, fac_in, fmeta,
    local_sem, r_send, r_recv, p_send, p_recv, l_send, l_recv, s_send, s_recv,
    a_send, a_recv, x_send, x_recv, m_send, m_recv, f_send, f_recv, g_send, g_recv,
):
    terms, nrb, rb, _ = right_ref.shape
    rows, cols = psi_ref.shape
    nd, nnz, bs = left_ref.shape[1], left_ref.shape[2], left_ref.shape[3]
    all_rows = 2 * rows
    z = lax.axis_index("op")
    c = lax.axis_index("blk")
    site = lax.axis_index("site")
    k = 2 * z + c
    ksib = 2 * z + 1 - c
    mine = pl.ds(pl.multiple_of(c * rows, rows), rows)
    theirs = pl.ds(pl.multiple_of((1 - c) * rows, rows), rows)

    def remote(src, dst, send, recv, device):
        return pltpu.make_async_remote_copy(
            src_ref=src, dst_ref=dst, send_sem=send, recv_sem=recv,
            device_id=device, device_id_type=MESH,
        )

    sibling = {"blk": 1 - c}
    across = {"site": 1 - site}
    diagonal = {"site": 1 - site, "blk": 1 - c}

    barrier = pltpu.get_barrier_semaphore()
    for off in range(1, n):
        pl.semaphore_signal(
            barrier, inc=1, device_id={"op": lax.rem(z + off, n)}, device_id_type=MESH
        )
    for dev in (sibling, across, diagonal):
        pl.semaphore_signal(barrier, inc=1, device_id=dev, device_id_type=MESH)

    own_l = pltpu.make_async_copy(left_ref, left, local_sem.at[3])
    own_p = pltpu.make_async_copy(
        psi_ref.at[:, pl.ds(pl.multiple_of(k * rb, rb), rb)], vec.at[mine], local_sem.at[1]
    )
    own_r = pltpu.make_async_copy(right_ref.at[:, k], r_all.at[z], local_sem.at[0])
    own_e = pltpu.make_async_copy(env_ref, env, local_sem.at[2])
    own_l.start()
    own_p.start()
    own_r.start()
    own_e.start()

    own_l.wait()
    diff = lax.broadcasted_iota(jnp.int32, (bs, all_rows), 1) - lax.broadcasted_iota(
        jnp.int32, (bs, all_rows), 0
    )
    for t in range(terms):
        for d in range(nd):
            total = jnp.zeros((bs, all_rows), F32)
            for j in range(nnz):
                place = jnp.where(diff == bs * src_ref[t, d, j], 1.0, 0.0).astype(BF16)
                total += jnp.dot(left[t, d, j], place, preferred_element_type=F32)
            at = pl.ds(pl.multiple_of(c * rows + d * bs, bs), bs)
            l_all[z, t, at, :] = total.astype(BF16)

    pl.semaphore_wait(barrier, n + 2)

    def hop(ref, way, o, h, step, send, recv):
        to = lax.rem(z + 1, n) if way == 0 else lax.rem(z + n - 1, n)
        return remote(ref(o, h), ref(o, h), send.at[way, step, h], recv.at[o, h], {"op": to})

    def start_line(ref, send, recv, pieces):
        for h in pieces:
            @pl.when(z + 1 < n)
            def _():
                hop(ref, 0, z, h, 0, send, recv).start()

            @pl.when(z > 0)
            def _():
                hop(ref, 1, z, h, 0, send, recv).start()

    def step_line(ref, send, recv, s, pieces, use):
        for h in pieces:
            @pl.when(z - s >= 0)
            def _():
                o = lax.rem(z - s + n, n)
                hop(ref, 0, o, h, 0, send, recv).wait_recv()
                if s < n - 1:
                    @pl.when(z + 1 < n)
                    def _():
                        hop(ref, 0, o, h, s, send, recv).start()
                use(o, h)

            @pl.when(z + s < n)
            def _():
                o = lax.rem(z + s, n)
                hop(ref, 1, o, h, 0, send, recv).wait_recv()
                if s < n - 1:
                    @pl.when(z > 0)
                    def _():
                        hop(ref, 1, o, h, s, send, recv).start()
                use(o, h)

    def arrived(s, use):
        @pl.when(z - s >= 0)
        def _():
            use(lax.rem(z - s + n, n))

        @pl.when(z + s < n)
        def _():
            use(lax.rem(z + s, n))

    def end_line(ref, send, recv, pieces):
        for s in range(n - 1):
            for h in pieces:
                @pl.when((z + 1 < n) & (z - s >= 0))
                def _():
                    hop(ref, 0, lax.rem(z - s + n, n), h, s, send, recv).wait_send()

                @pl.when((z > 0) & (z + s < n))
                def _():
                    hop(ref, 1, lax.rem(z + s, n), h, s, send, recv).wait_send()

    def l_slot(o, t):
        return l_all.at[o, t, mine, :]

    def to_sibling(o, t):
        return remote(l_slot(o, t), l_slot(o, t), s_send.at[o, t], s_recv.at[o, t], sibling)

    def partner(i):
        falling = jnp.where(n - 1 - i > z, n - 1 - i, n - 2 - i)
        rising = jnp.where(i >= z, i + 1, i)
        return lax.rem(jnp.where(z < n // 2, falling, rising) + n, n)

    def r_copy(i, t):
        dest = partner(i)
        return remote(
            right_ref.at[t, 2 * dest + c], r_all.at[z, t], r_send.at[i, t], r_recv.at[z, t],
            {"op": dest},
        )

    every = range(terms)
    start_line(l_slot, l_send, l_recv, every)
    p_copy = remote(
        psi_ref.at[:, pl.ds(pl.multiple_of(ksib * rb, rb), rb)], vec.at[mine],
        p_send, p_recv, sibling,
    )
    p_copy.start()
    for t in every:
        to_sibling(z, t).start()
    work = [(i, t) for i in range(n - 1) for t in every]
    share = [len(work) * s // n for s in range(1, n)]
    done = 0
    for s in range(1, n):
        for i, t in work[done:share[s - 1]]:
            r_copy(i, t).start()
        done = share[s - 1]
        step_line(l_slot, l_send, l_recv, s, every, lambda o, t: to_sibling(o, t).start())
    for i, t in work[done:]:
        r_copy(i, t).start()

    own_p.wait()
    p_copy.wait()
    own_r.wait()

    def product(o, t):
        moved = jnp.dot(vec[...], r_all[o, t], preferred_element_type=F32).astype(BF16)
        return jnp.dot(l_all[o, t], moved, preferred_element_type=F32)

    image = jnp.zeros((all_rows, rb), F32)
    for i in range(-1, n - 1):
        o = z if i < 0 else partner(i)
        for t in every:
            to_sibling(o, t).wait_recv()
            if i >= 0:
                remote(
                    right_ref.at[t, k], r_all.at[o, t], r_send.at[0, 0], r_recv.at[o, t],
                    {"op": o},
                ).wait_recv()
            image = image + product(o, t)

    exponent = jnp.zeros((1, 1), F32)

    def settle(image, exponent):
        top = jnp.max(jnp.abs(image), axis=(0, 1), keepdims=True)
        e = jnp.where(top > 0.0, jnp.clip(jnp.floor(jnp.log2(top)), -100.0, 100.0), 0.0)
        return image * jnp.exp2(-e), exponent + e

    for step in range(1, ITERS):
        image, exponent = settle(image, exponent)
        vec[...] = image.astype(BF16)
        image = jnp.zeros((all_rows, rb), F32)
        for o in range(n):
            for t in every:
                image = image + product(o, t)
    image, exponent = settle(image, exponent)
    vec[...] = image.astype(BF16)

    x_copy = remote(vec.at[theirs, :], tail.at[z, c], x_send.at[0], x_recv.at[0], sibling)
    x_copy.start()
    tail[z, c] = vec[mine, :]

    def a_slot(o, h):
        return tail.at[o, c if h == 0 else 1 - c]

    start_line(a_slot, a_send, a_recv, (0,))
    square = jnp.sum(image * image, axis=(0, 1), keepdims=True)
    lane = lax.broadcasted_iota(jnp.int32, (8, 128), 1)
    meta[z, c] = jnp.where(lane == 0, jnp.broadcast_to(exponent, (8, 128)),
                           jnp.broadcast_to(square, (8, 128)))
    xm_copy = remote(meta.at[z, c], meta.at[z, c], x_send.at[1], x_recv.at[1], sibling)
    xm_copy.start()
    x_copy.wait()
    start_line(a_slot, a_send, a_recv, (1,))
    xm_copy.wait()

    def m_copy(off):
        return remote(
            meta.at[z], meta.at[z], m_send.at[off], m_recv.at[z], {"op": lax.rem(z + off, n)}
        )

    for off in range(1, n):
        m_copy(off).start()

    step_line(a_slot, a_send, a_recv, 1, (0, 1), lambda o, h: None)
    for off in range(1, n):
        o = lax.rem(z + off, n)
        remote(
            meta.at[o], meta.at[o], m_send.at[0], m_recv.at[o], {"op": o}
        ).wait_recv()

    exps = [meta[o // 2, o % 2][0:1, 0:1] for o in range(2 * n)]
    sqs = [meta[o // 2, o % 2][0:1, 1:2] for o in range(2 * n)]
    low = jnp.full((1, 1), -1.0e4, F32)
    big = low
    for e, q in zip(exps, sqs):
        big = jnp.maximum(big, jnp.where(q > 0.0, e, low))
    ww = jnp.zeros((1, 1), F32)
    weights = []
    for e, q in zip(exps, sqs):
        r = jnp.where(q > 0.0, jnp.exp2(jnp.maximum(e - big, -120.0)), 0.0)
        weights.append(r)
        ww = ww + q * r * r
    unit = jnp.sqrt(float(all_rows * cols) / ww)
    for o, r in enumerate(weights):
        rel[o] = jnp.broadcast_to(r * unit, (8, 128))

    own_e.wait()
    total_fac[...] = jnp.zeros(out_ref.shape, F32)

    def finish(o):
        part = total_fac[...]
        for half in range(2):
            scale = rel[2 * o + half][0:1, 0:1]
            block = (tail[o, half].astype(F32) * scale).astype(BF16)
            at = pl.ds(pl.multiple_of((2 * o + half) * rb, rb), rb)
            amp_ref[:, at] = block
            part = part + jnp.dot(block, env[at, :], preferred_element_type=F32)
        total_fac[...] = part

    finish(z)
    arrived(1, finish)
    for s in range(2, n):
        step_line(a_slot, a_send, a_recv, s, (0, 1), lambda o, h: None)
        arrived(s, finish)

    fac[...] = total_fac[...].astype(BF16)
    f_copy = remote(fac, fac_in, f_send, f_recv, across)
    f_copy.start()
    rounded = fac[...].astype(F32)
    fsq = jnp.sum(rounded * rounded, axis=(0, 1), keepdims=True)
    fmeta[0] = jnp.broadcast_to(fsq, (8, 128))
    g_near = remote(fmeta.at[0], fmeta.at[1], g_send.at[0], g_recv.at[0], across)
    g_far = remote(fmeta.at[0], fmeta.at[2], g_send.at[1], g_recv.at[1], diagonal)
    g_near.start()
    g_far.start()

    for i, t in work:
        r_copy(i, t).wait_send()
    for off in range(1, n):
        m_copy(off).wait_send()
    end_line(l_slot, l_send, l_recv, every)
    end_line(a_slot, a_send, a_recv, (0, 1))
    for o in range(n):
        for t in every:
            to_sibling(o, t).wait_send()
    eye = jnp.where(
        lax.broadcasted_iota(jnp.int32, out_ref.shape, 0) + c * rows
        == lax.broadcasted_iota(jnp.int32, out_ref.shape, 1), 1.0, 0.0,
    )
    first = jnp.full(out_ref.shape, site, jnp.int32) == 0
    g_near.wait()
    g_far.wait()
    f_copy.wait()
    total = fmeta[1][0:1, 0:1] + fmeta[2][0:1, 0:1]
    earlier = fac_in[...].astype(F32) * lax.rsqrt(total / float(all_rows * out_ref.shape[1]))
    out_ref[...] = jnp.where(first, eye, earlier)


def column_plan(psi, right_ops, left_blocks, sources, env_basis):
    n = lax.axis_size("op")
    rows, cols = psi.shape[1], psi.shape[2]
    terms, nrb, rb = right_ops.shape[1], right_ops.shape[2], right_ops.shape[3]
    width = env_basis.shape[2]
    dma = pltpu.SemaphoreType.DMA
    hbm = pl.BlockSpec(memory_space=pltpu.HBM)
    vmem = pl.BlockSpec(memory_space=pltpu.VMEM)
    amplitudes, environment = pl.pallas_call(
        functools.partial(column_kernel, n),
        out_shape=(
            jax.ShapeDtypeStruct((rows, cols), BF16),
            jax.ShapeDtypeStruct((rows, width), F32),
        ),
        in_specs=[pl.BlockSpec(memory_space=pltpu.SMEM), hbm, hbm, hbm, hbm],
        out_specs=(vmem, vmem),
        scratch_shapes=[
            pltpu.VMEM((n, terms, rb, rb), BF16),
            pltpu.VMEM((n, terms, 2 * rows, 2 * rows), BF16),
            pltpu.VMEM((2 * rows, rb), BF16),
            pltpu.VMEM((cols, width), BF16),
            pltpu.VMEM(left_blocks.shape[1:], BF16),
            pltpu.VMEM((n, 2, rows, rb), BF16),
            pltpu.VMEM((n, 2, 8, 128), F32),
            pltpu.VMEM((2 * n, 8, 128), F32),
            pltpu.VMEM((rows, width), F32),
            pltpu.VMEM((rows, width), BF16),
            pltpu.VMEM((rows, width), BF16),
            pltpu.VMEM((3, 8, 128), F32),
            dma((4,)),
            dma((n, terms)), dma((n, terms)), dma, dma,
            dma((2, n, terms)), dma((n, terms)), dma((n, terms)), dma((n, terms)),
            dma((2, n, 2)), dma((n, 2)), dma((2,)), dma((2,)), dma((n,)), dma((n,)),
            dma, dma, dma((2,)), dma((2,)),
        ],
        compiler_params=pltpu.CompilerParams(
            collective_id=0, has_side_effects=True, vmem_limit_bytes=53 * 1024 * 1024
        ),
    )(sources[0], psi[0], right_ops[0], left_blocks[0], env_basis[0])
    return (amplitudes[None], environment[None])


def on_device(psi, right_ops, left_blocks, sources, env_basis):
    owners = lax.axis_size("op") * lax.axis_size("blk")
    fits = (
        owners == right_ops.shape[2]
        and lax.axis_size("blk") == 2
        and lax.axis_size("site") == 2
        and psi.shape[0] == 1
        and env_basis.shape[2] == 2 * psi.shape[1]
    )
    plan = column_plan if fits else general_plan
    return plan(psi, right_ops, left_blocks, sources, env_basis)


def solution(mesh):
    placed = (
        P(("group", "site"), "blk", None),
        P(("group", "site"), "op", None, None, None),
        P(("group", "site"), "op", "blk", None, None, None),
        P(("group", "site"), "op", "blk", None),
        P(("group", "site"), None, None),
    )
    return jax.shard_map(
        on_device,
        mesh=mesh,
        in_specs=placed,
        out_specs=(P(("group", "site"), "blk", None), P(("group", "site"), "blk", None)),
        check_vma=False,
    )
```

time: 71.4 us -> 60.4 us (0.85)
  Pallas kernels: 63.4 us -> 57.4 us
  local copies, waits for them, and re-layouts: 7.02 us -> 2.13 us
    pallas_call x1, Pallas kernels: 63.4 us -> 57.4 us  [column_plan(): pl.pallas_call(functools.partial(column_kernel, n), out_shape=(jax.ShapeD...]
    unnamed x12 -> x4, local copies, waits for them, and re-layouts: 7.02 us -> 2.13 us
where the time goes in v2:
time: 60.4 us; the launch traced here: 60.2 us
  Pallas kernels  57.4 us (95%)
  local copies, waits for them, and re-layouts  2.13 us (4%)
  between operations  0.65 us (1%)
    pallas_call x1, Pallas kernels, column_plan(): pl.pallas_call(functools.partial(column_kernel, n), out_shape=(jax.ShapeD...  57.4 us
    unnamed x4, local copies, waits for them, and re-layouts  2.13 us

profile of v2, /device:TPU:0, one launch (start us, length us, event | category | flops | bytes accessed | tf_op | source)
XLA Modules:
  0.0 60.2 jit_solution(18206904259404651375)
XLA Ops:
  0.6 0.0 copy-start
  0.6 0.7 %copy-done = s32[1,2,2,8]{3,2,1,0:T(2,128)S(1)} copy-done((s32[1,2,2,8]{3,2,1,0:T(2,128)S(1)}, s32[1,2,2,8]{3,2,1,0:T(2,128)}, u32[]{:S(2)}) %copy-start) | copy-done | bytes 152
  1.3 57.4 %shard_map.68 = (bf16[128,2048]{1,0:T(8,128)(2,1)S(1)}, f32[128,256]{1,0:T(8,128)S(1)}) custom-call(s32[2,2,8]{2,1,0:T(2,128)S(1)} %bitcast.9, bf16[128,2048]{1,0:T(8,128)(2,1)} %bitcast.12, bf16[2,8,256,256]{3,2,1,0:T(8,128)(2,1)} %bitcast.10, bf16[2,2,8,64,64]{4,3,2,1,0:T(8,128)(2,1)} %bitcast.13, bf16[2048,256]{1,0:T(8,128)(2,1)} %bitcast.11), custom_call_target="tpu_custom_call" | custom-call | tf_op jit(solution)/shard_map/pallas_call | solution.py:378
  58.7 0.8 %copy.9 = bf16[1,128,2048]{2,1,0:T(8,128)(2,1)} copy(bf16[1,128,2048]{2,1,0:T(8,128)(2,1)S(1)} %bitcast.7) | data formatting | bytes 1048576
  59.5 0.7 %copy.10 = f32[1,128,256]{2,1,0:T(8,128)} copy(f32[1,128,256]{2,1,0:T(8,128)S(1)} %bitcast.8) | data formatting | bytes 262144
Async XLA Ops:
  0.6 0.7 %copy-start = (s32[1,2,2,8]{3,2,1,0:T(2,128)S(1)}, s32[1,2,2,8]{3,2,1,0:T(2,128)}, u32[]{:S(2)}) copy-start(s32[1,2,2,8]{3,2,1,0:T(2,128)} %param.8) | copy-start | bytes 388

commit v3 on v2

--- a/solution.py
+++ b/solution.py
@@ -75,7 +75,7 @@
 
 def column_kernel(
     n, src_ref, psi_ref, right_ref, left_ref, env_ref, amp_ref, out_ref,
-    r_all, l_all, vec, env, left, tail, meta, rel, total_fac, fac, fac_in, fmeta,
+    src, r_all, l_all, vec, env, left, tail, meta, rel, total_fac, fac, fac_in, fmeta,
     local_sem, r_send, r_recv, p_send, p_recv, l_send, l_recv, s_send, s_recv,
     a_send, a_recv, x_send, x_recv, m_send, m_recv, f_send, f_recv, g_send, g_recv,
 ):
@@ -115,11 +115,14 @@
     )
     own_r = pltpu.make_async_copy(right_ref.at[:, k], r_all.at[z], local_sem.at[0])
     own_e = pltpu.make_async_copy(env_ref, env, local_sem.at[2])
+    own_s = pltpu.make_async_copy(src_ref, src, local_sem.at[4])
+    own_s.start()
     own_l.start()
     own_p.start()
     own_r.start()
     own_e.start()
 
+    own_s.wait()
     own_l.wait()
     diff = lax.broadcasted_iota(jnp.int32, (bs, all_rows), 1) - lax.broadcasted_iota(
         jnp.int32, (bs, all_rows), 0
@@ -128,7 +131,7 @@
         for d in range(nd):
             total = jnp.zeros((bs, all_rows), F32)
             for j in range(nnz):
-                place = jnp.where(diff == bs * src_ref[t, d, j], 1.0, 0.0).astype(BF16)
+                place = jnp.where(diff == bs * src[t, d, j], 1.0, 0.0).astype(BF16)
                 total += jnp.dot(left[t, d, j], place, preferred_element_type=F32)
             at = pl.ds(pl.multiple_of(c * rows + d * bs, bs), bs)
             l_all[z, t, at, :] = total.astype(BF16)
@@ -218,7 +221,7 @@
     p_copy.start()
     for t in every:
         to_sibling(z, t).start()
-    work = [(i, t) for i in range(n - 1) for t in every]
+    work = [(i, t) for t in every for i in range(n - 1)]
     share = [len(work) * s // n for s in range(1, n)]
     done = 0
     for s in range(1, n):
@@ -260,9 +263,13 @@
         image, exponent = settle(image, exponent)
         vec[...] = image.astype(BF16)
         image = jnp.zeros((all_rows, rb), F32)
+        v = vec[...]
         for o in range(n):
-            for t in every:
-                image = image + product(o, t)
+            moved = [jnp.dot(v, r_all[o, t], preferred_element_type=F32).astype(BF16)
+                     for t in every]
+            image = image + jnp.dot(
+                jnp.concatenate([l_all[o, t] for t in every], axis=1),
+                jnp.concatenate(moved, axis=0), preferred_element_type=F32)
     image, exponent = settle(image, exponent)
     vec[...] = image.astype(BF16)
 
@@ -381,9 +388,10 @@
             jax.ShapeDtypeStruct((rows, cols), BF16),
             jax.ShapeDtypeStruct((rows, width), F32),
         ),
-        in_specs=[pl.BlockSpec(memory_space=pltpu.SMEM), hbm, hbm, hbm, hbm],
+        in_specs=[hbm, hbm, hbm, hbm, hbm],
         out_specs=(vmem, vmem),
         scratch_shapes=[
+            pltpu.SMEM(sources.shape[1:], jnp.int32),
             pltpu.VMEM((n, terms, rb, rb), BF16),
             pltpu.VMEM((n, terms, 2 * rows, 2 * rows), BF16),
             pltpu.VMEM((2 * rows, rb), BF16),
@@ -396,7 +404,7 @@
             pltpu.VMEM((rows, width), BF16),
             pltpu.VMEM((rows, width), BF16),
             pltpu.VMEM((3, 8, 128), F32),
-            dma((4,)),
+            dma((5,)),
             dma((n, terms)), dma((n, terms)), dma, dma,
             dma((2, n, terms)), dma((n, terms)), dma((n, terms)), dma((n, terms)),
             dma((2, n, 2)), dma((n, 2)), dma((2,)), dma((2,)), dma((n,)), dma((n,)),

time: 60.4 us -> 57.5 us (0.952)
  Pallas kernels: 57.4 us -> 54.5 us
    pallas_call x1, Pallas kernels: 57.4 us -> 54.5 us  [column_plan(): pl.pallas_call(functools.partial(column_kernel, n), out_shape=(jax.ShapeD...]
where the time goes in v3:
time: 57.5 us; the launch traced here: 57.3 us
  Pallas kernels  54.5 us (95%)
  local copies, waits for them, and re-layouts  2.13 us (4%)
  between operations  0.65 us (1%)
    pallas_call x1, Pallas kernels, column_plan(): pl.pallas_call(functools.partial(column_kernel, n), out_shape=(jax.ShapeD...  54.5 us
    unnamed x4, local copies, waits for them, and re-layouts  2.13 us

profile of v3, /device:TPU:0, one launch (start us, length us, event | category | flops | bytes accessed | tf_op | source)
XLA Modules:
  0.0 57.3 jit_solution(16823793101841547107)
XLA Ops:
  0.6 0.0 copy-start
  0.6 0.7 %copy-done = s32[1,2,2,8]{3,2,1,0:T(2,128)S(1)} copy-done((s32[1,2,2,8]{3,2,1,0:T(2,128)S(1)}, s32[1,2,2,8]{3,2,1,0:T(2,128)}, u32[]{:S(2)}) %copy-start) | copy-done | bytes 152
  1.3 54.5 %shard_map.68 = (bf16[128,2048]{1,0:T(8,128)(2,1)S(1)}, f32[128,256]{1,0:T(8,128)S(1)}) custom-call(s32[2,2,8]{2,1,0:T(2,128)S(1)} %bitcast.9, bf16[128,2048]{1,0:T(8,128)(2,1)} %bitcast.12, bf16[2,8,256,256]{3,2,1,0:T(8,128)(2,1)} %bitcast.10, bf16[2,2,8,64,64]{4,3,2,1,0:T(8,128)(2,1)} %bitcast.13, bf16[2048,256]{1,0:T(8,128)(2,1)} %bitcast.11), custom_call_target="tpu_custom_call" | custom-call | tf_op jit(solution)/shard_map/pallas_call | solution.py:385
  55.8 0.8 %copy.9 = bf16[1,128,2048]{2,1,0:T(8,128)(2,1)} copy(bf16[1,128,2048]{2,1,0:T(8,128)(2,1)S(1)} %bitcast.7) | data formatting | bytes 1048576
  56.6 0.7 %copy.10 = f32[1,128,256]{2,1,0:T(8,128)} copy(f32[1,128,256]{2,1,0:T(8,128)S(1)} %bitcast.8) | data formatting | bytes 262144
Async XLA Ops:
  0.6 0.7 %copy-start = (s32[1,2,2,8]{3,2,1,0:T(2,128)S(1)}, s32[1,2,2,8]{3,2,1,0:T(2,128)}, u32[]{:S(2)}) copy-start(s32[1,2,2,8]{3,2,1,0:T(2,128)} %param.8) | copy-start | bytes 388

commit v4 on v3

--- a/solution.py
+++ b/solution.py
@@ -278,9 +278,9 @@
     tail[z, c] = vec[mine, :]
 
     def a_slot(o, h):
-        return tail.at[o, c if h == 0 else 1 - c]
-
-    start_line(a_slot, a_send, a_recv, (0,))
+        return tail.at[o, c if h < 2 else 1 - c, pl.ds((h % 2) * (rows // 2), rows // 2)]
+
+    start_line(a_slot, a_send, a_recv, (0, 1))
     square = jnp.sum(image * image, axis=(0, 1), keepdims=True)
     lane = lax.broadcasted_iota(jnp.int32, (8, 128), 1)
     meta[z, c] = jnp.where(lane == 0, jnp.broadcast_to(exponent, (8, 128)),
@@ -288,7 +288,7 @@
     xm_copy = remote(meta.at[z, c], meta.at[z, c], x_send.at[1], x_recv.at[1], sibling)
     xm_copy.start()
     x_copy.wait()
-    start_line(a_slot, a_send, a_recv, (1,))
+    start_line(a_slot, a_send, a_recv, (2, 3))
     xm_copy.wait()
 
     def m_copy(off):
@@ -299,7 +299,7 @@
     for off in range(1, n):
         m_copy(off).start()
 
-    step_line(a_slot, a_send, a_recv, 1, (0, 1), lambda o, h: None)
+    step_line(a_slot, a_send, a_recv, 1, range(4), lambda o, h: None)
     for off in range(1, n):
         o = lax.rem(z + off, n)
         remote(
@@ -338,7 +338,7 @@
     finish(z)
     arrived(1, finish)
     for s in range(2, n):
-        step_line(a_slot, a_send, a_recv, s, (0, 1), lambda o, h: None)
+        step_line(a_slot, a_send, a_recv, s, range(4), lambda o, h: None)
         arrived(s, finish)
 
     fac[...] = total_fac[...].astype(BF16)
@@ -357,7 +357,7 @@
     for off in range(1, n):
         m_copy(off).wait_send()
     end_line(l_slot, l_send, l_recv, every)
-    end_line(a_slot, a_send, a_recv, (0, 1))
+    end_line(a_slot, a_send, a_recv, range(4))
     for o in range(n):
         for t in every:
             to_sibling(o, t).wait_send()
@@ -407,7 +407,7 @@
             dma((5,)),
             dma((n, terms)), dma((n, terms)), dma, dma,
             dma((2, n, terms)), dma((n, terms)), dma((n, terms)), dma((n, terms)),
-            dma((2, n, 2)), dma((n, 2)), dma((2,)), dma((2,)), dma((n,)), dma((n,)),
+            dma((2, n, 4)), dma((n, 4)), dma((2,)), dma((2,)), dma((n,)), dma((n,)),
             dma, dma, dma((2,)), dma((2,)),
         ],
         compiler_params=pltpu.CompilerParams(

time: 57.5 us -> 56.9 us (0.990)
  Pallas kernels: 54.5 us -> 53.9 us
    pallas_call x1, Pallas kernels: 54.5 us -> 53.9 us  [column_plan(): pl.pallas_call(functools.partial(column_kernel, n), out_shape=(jax.ShapeD...]
where the time goes in v4:
time: 56.9 us; the launch traced here: 56.7 us
  Pallas kernels  53.9 us (95%)
  local copies, waits for them, and re-layouts  2.13 us (4%)
  between operations  0.65 us (1%)
    pallas_call x1, Pallas kernels, column_plan(): pl.pallas_call(functools.partial(column_kernel, n), out_shape=(jax.ShapeD...  53.9 us
    unnamed x4, local copies, waits for them, and re-layouts  2.13 us

profile of v4, /device:TPU:0, one launch (start us, length us, event | category | flops | bytes accessed | tf_op | source)
XLA Modules:
  0.0 56.7 jit_solution(3046334926015106091)
XLA Ops:
  0.6 0.0 copy-start
  0.6 0.7 %copy-done = s32[1,2,2,8]{3,2,1,0:T(2,128)S(1)} copy-done((s32[1,2,2,8]{3,2,1,0:T(2,128)S(1)}, s32[1,2,2,8]{3,2,1,0:T(2,128)}, u32[]{:S(2)}) %copy-start) | copy-done | bytes 152
  1.3 53.9 %shard_map.68 = (bf16[128,2048]{1,0:T(8,128)(2,1)S(1)}, f32[128,256]{1,0:T(8,128)S(1)}) custom-call(s32[2,2,8]{2,1,0:T(2,128)S(1)} %bitcast.9, bf16[128,2048]{1,0:T(8,128)(2,1)} %bitcast.12, bf16[2,8,256,256]{3,2,1,0:T(8,128)(2,1)} %bitcast.10, bf16[2,2,8,64,64]{4,3,2,1,0:T(8,128)(2,1)} %bitcast.13, bf16[2048,256]{1,0:T(8,128)(2,1)} %bitcast.11), custom_call_target="tpu_custom_call" | custom-call | tf_op jit(solution)/shard_map/pallas_call | solution.py:385
  55.2 0.8 %copy.9 = bf16[1,128,2048]{2,1,0:T(8,128)(2,1)} copy(bf16[1,128,2048]{2,1,0:T(8,128)(2,1)S(1)} %bitcast.7) | data formatting | bytes 1048576
  56.0 0.7 %copy.10 = f32[1,128,256]{2,1,0:T(8,128)} copy(f32[1,128,256]{2,1,0:T(8,128)S(1)} %bitcast.8) | data formatting | bytes 262144
Async XLA Ops:
  0.6 0.7 %copy-start = (s32[1,2,2,8]{3,2,1,0:T(2,128)S(1)}, s32[1,2,2,8]{3,2,1,0:T(2,128)}, u32[]{:S(2)}) copy-start(s32[1,2,2,8]{3,2,1,0:T(2,128)} %param.8) | copy-start | bytes 388

commit v5 on v4

--- a/solution.py
+++ b/solution.py
@@ -262,14 +262,12 @@
     for step in range(1, ITERS):
         image, exponent = settle(image, exponent)
         vec[...] = image.astype(BF16)
-        image = jnp.zeros((all_rows, rb), F32)
         v = vec[...]
-        for o in range(n):
-            moved = [jnp.dot(v, r_all[o, t], preferred_element_type=F32).astype(BF16)
-                     for t in every]
-            image = image + jnp.dot(
-                jnp.concatenate([l_all[o, t] for t in every], axis=1),
-                jnp.concatenate(moved, axis=0), preferred_element_type=F32)
+        moved = [jnp.dot(v, r_all[o, t], preferred_element_type=F32).astype(BF16)
+                 for o in range(n) for t in every]
+        image = jnp.dot(
+            jnp.concatenate([l_all[o, t] for o in range(n) for t in every], axis=1),
+            jnp.concatenate(moved, axis=0), preferred_element_type=F32)
     image, exponent = settle(image, exponent)
     vec[...] = image.astype(BF16)
 

time: 56.9 us -> 56.7 us (level)
  no operation moved by 1% of the time
where the time goes in v5:
time: 56.7 us; the launch traced here: 56.5 us
  Pallas kernels  53.7 us (95%)
  local copies, waits for them, and re-layouts  2.13 us (4%)
  between operations  0.65 us (1%)
    pallas_call x1, Pallas kernels, column_plan(): pl.pallas_call(functools.partial(column_kernel, n), out_shape=(jax.ShapeD...  53.7 us
    unnamed x4, local copies, waits for them, and re-layouts  2.13 us

profile of v5, /device:TPU:0, one launch (start us, length us, event | category | flops | bytes accessed | tf_op | source)
XLA Modules:
  0.0 56.5 jit_solution(6577566090724006783)
XLA Ops:
  0.6 0.0 copy-start
  0.6 0.7 %copy-done = s32[1,2,2,8]{3,2,1,0:T(2,128)S(1)} copy-done((s32[1,2,2,8]{3,2,1,0:T(2,128)S(1)}, s32[1,2,2,8]{3,2,1,0:T(2,128)}, u32[]{:S(2)}) %copy-start) | copy-done | bytes 152
  1.3 53.7 %shard_map.68 = (bf16[128,2048]{1,0:T(8,128)(2,1)S(1)}, f32[128,256]{1,0:T(8,128)S(1)}) custom-call(s32[2,2,8]{2,1,0:T(2,128)S(1)} %bitcast.9, bf16[128,2048]{1,0:T(8,128)(2,1)} %bitcast.12, bf16[2,8,256,256]{3,2,1,0:T(8,128)(2,1)} %bitcast.10, bf16[2,2,8,64,64]{4,3,2,1,0:T(8,128)(2,1)} %bitcast.13, bf16[2048,256]{1,0:T(8,128)(2,1)} %bitcast.11), custom_call_target="tpu_custom_call" | custom-call | tf_op jit(solution)/shard_map/pallas_call | solution.py:383
  55.0 0.8 %copy.9 = bf16[1,128,2048]{2,1,0:T(8,128)(2,1)} copy(bf16[1,128,2048]{2,1,0:T(8,128)(2,1)S(1)} %bitcast.7) | data formatting | bytes 1048576
  55.8 0.7 %copy.10 = f32[1,128,256]{2,1,0:T(8,128)} copy(f32[1,128,256]{2,1,0:T(8,128)S(1)} %bitcast.8) | data formatting | bytes 262144
Async XLA Ops:
  0.6 0.7 %copy-start = (s32[1,2,2,8]{3,2,1,0:T(2,128)S(1)}, s32[1,2,2,8]{3,2,1,0:T(2,128)}, u32[]{:S(2)}) copy-start(s32[1,2,2,8]{3,2,1,0:T(2,128)} %param.8) | copy-start | bytes 388
